TPU v7x, 512 devices: a whole 4x4x16 slice. The times are simulated.
512 devices in a mesh: src: 16 (over z), tgt: 32 (over y, x, core).
Axes of the slice: x: 4, y: 4, z: 16, core: 2. Of those that a mesh axis runs over, the one named last changes fastest.
Arguments:
- source_latents: float32 [32768, 64], P(('src', 'tgt')), may hold values from -20 to 20
- target_latents: float32 [32768, 64], P('tgt'), may hold values from -20 to 20
Outputs:
- source_potential: float32 [32768], P('src')
- target_potential: float32 [32768], P('tgt')
- row_mass: float32 [32768], P('src')
All inputs are finite; a program needn't handle non-finite values.
Results may differ from a plain program's by a relative error of at most 0.00035.
Values sent between devices are 32-bit elements; how exact they have to be, the bound alone decides.
A program may use at most 64 MiB of HBM per device.

v0:
```python
import math

import jax
import jax.numpy as jnp
from jax import lax
from jax.sharding import PartitionSpec as P

ITERS = 4


def row_lse(scores):
    highest = lax.pmax(jnp.max(scores, 1), "tgt")
    total = lax.psum(jnp.sum(jnp.exp(scores - highest[:, None]), 1), "tgt")
    return highest + jnp.log(total)


def col_lse(scores):
    highest = lax.pmax(jnp.max(scores, 0), "src")
    total = lax.psum(jnp.sum(jnp.exp(scores - highest[None, :]), 0), "src")
    return highest + jnp.log(total)


def body(source_latents, target_latents):
    n_source = source_latents.shape[0] * lax.axis_size("tgt") * lax.axis_size("src")
    n_target = target_latents.shape[0] * lax.axis_size("tgt")
    rows = lax.all_gather(source_latents, "tgt", axis=0, tiled=True)
    src_norms = jnp.sum(rows * rows, 1)
    tgt_norms = jnp.sum(target_latents * target_latents, 1)
    cross = lax.dot_general(
        rows,
        target_latents,
        (((1,), (1,)), ((), ())),
        precision=lax.Precision.HIGHEST,
        preferred_element_type=jnp.float32,
    )
    cost = src_norms[:, None] + tgt_norms[None, :] - 2.0 * cross
    mean_cost = lax.psum(jnp.sum(cost), ("src", "tgt")) / (n_source * n_target)
    regular = 0.05 * mean_cost
    scaled = cost / regular
    log_source = -math.log(n_source)
    log_target = -math.log(n_target)
    potential_v = jnp.zeros((target_latents.shape[0],), jnp.float32)
    potential_u = jnp.zeros((rows.shape[0],), jnp.float32)
    for step in range(ITERS):
        potential_u = log_source - row_lse(potential_v[None, :] - scaled)
        potential_v = log_target - col_lse(potential_u[:, None] - scaled)
    updated = log_source - row_lse(potential_v[None, :] - scaled)
    row_mass = jnp.exp(potential_u - updated)
    return (potential_u, potential_v, row_mass)


def solution(mesh):
    in_specs = (P(("src", "tgt"), None), P("tgt", None))
    out_specs = (P("src"), P("tgt"), P("src"))
    return jax.shard_map(body, mesh=mesh, in_specs=in_specs, out_specs=out_specs, check_vma=False)
```

profile of v0, /device:TPU:1, one launch (start us, length us, event | category | flops | bytes accessed | tf_op | source)
XLA Modules:
  0.0 1090.3 jit_solution(12219991162571266301)
XLA Ops:
  1.6 29.4 %all_gather.3 = f32[2048,64]{1,0:T(8,128)S(1)} all-gather(f32[64,64]{1,0:T(8,128)} %param.2), channel_id=1, replica_groups=mesh['src'=16,'tgt'=32] {'tgt'}, dimensions={0}, use_global_device_ids=true | all-gather | bytes 540672 | tf_op jit(solution)/shard_map/all_gather | solution.py:26
  31.3 11.7 %fusion.1 = (f32[]{:T(128)}, f32[2048,1024]{0,1:T(8,128)}) fusion(f32[1024]{0:T(1024)S(1)} %multiply_reduce_fusion.1, f32[2048]{0:T(1024)S(1)} %multiply_reduce_fusion, f32[2048,64]{1,0:T(8,128)S(1)} %all_gather.3, f32[1024,64]{0,1:T(8,128)} %param.3), kind=kOutput, calls=%fused_computation.20 | convolution fusion | flops 1619001344 | bytes 9187332 | tf_op jit(solution)/shard_map/dot_general | solution.py:29
  43.0 104.9 %psum.70 = f32[]{:T(128)} all-reduce(f32[]{:T(128)} %get-tuple-element.5), channel_id=1, replica_groups=mesh['src'=16,'tgt'=32] {'src','tgt'}, use_global_device_ids=true, to_apply=%region_3.0 | all-reduce | flops 1 | bytes 8 | tf_op jit(solution)/shard_map/psum | solution.py:37
  148.6 6.6 subtract_reduce_fusion.8
  155.2 63.6 %pmax.63 = f32[2048]{0:T(1024)S(1)} all-reduce(f32[2048]{0:T(1024)S(1)} %get-tuple-element.3), channel_id=1, replica_groups=mesh['src'=16,'tgt'=32] {'tgt'}, use_global_device_ids=true, to_apply=%region_5.0 | all-reduce | flops 2048 | bytes 16384 | tf_op jit(solution)/shard_map/pmax | solution.py:12
  218.8 4.8 exponential_reduce_fusion.8
  223.6 65.0 %psum.71 = f32[2048]{0:T(1024)S(1)} all-reduce(f32[2048]{0:T(1024)S(1)} %exponential_reduce_fusion.8), channel_id=1, replica_groups=mesh['src'=16,'tgt'=32] {'tgt'}, use_global_device_ids=true, to_apply=%region_7.0 | all-reduce | flops 2048 | bytes 16384 | tf_op jit(solution)/shard_map/psum | solution.py:13
  292.7 21.0 %pmax.64 = f32[1024]{0:T(1024)S(1)} all-reduce(f32[1024]{0:T(1024)S(1)} %subtract_reduce_fusion.7), channel_id=1, replica_groups=mesh['src'=16,'tgt'=32] {'src'}, use_global_device_ids=true, to_apply=%region_9.0 | all-reduce | flops 1024 | bytes 8192 | tf_op jit(solution)/shard_map/pmax | solution.py:18
  313.7 4.4 exponential_reduce_fusion.7
  318.1 21.0 %psum.72 = f32[1024]{0:T(1024)S(1)} all-reduce(f32[1024]{0:T(1024)S(1)} %exponential_reduce_fusion.7), channel_id=1, replica_groups=mesh['src'=16,'tgt'=32] {'src'}, use_global_device_ids=true, to_apply=%region_11.0 | all-reduce | flops 1024 | bytes 8192 | tf_op jit(solution)/shard_map/psum | solution.py:19
  343.1 77.9 %pmax.65 = f32[2048]{0:T(1024)S(1)} all-reduce(f32[2048]{0:T(1024)S(1)} %subtract_reduce_fusion.6), channel_id=1, replica_groups=mesh['src'=16,'tgt'=32] {'tgt'}, use_global_device_ids=true, to_apply=%region_13.0 | all-reduce | flops 2048 | bytes 16384 | tf_op jit(solution)/shard_map/pmax | solution.py:12
  421.0 4.3 exponential_reduce_fusion.6
  425.3 63.7 %psum.73 = f32[2048]{0:T(1024)S(1)} all-reduce(f32[2048]{0:T(1024)S(1)} %exponential_reduce_fusion.6), channel_id=1, replica_groups=mesh['src'=16,'tgt'=32] {'tgt'}, use_global_device_ids=true, to_apply=%region_15.0 | all-reduce | flops 2048 | bytes 16384 | tf_op jit(solution)/shard_map/psum | solution.py:13
  493.1 21.0 %pmax.66 = f32[1024]{0:T(1024)S(1)} all-reduce(f32[1024]{0:T(1024)S(1)} %subtract_reduce_fusion.5), channel_id=1, replica_groups=mesh['src'=16,'tgt'=32] {'src'}, use_global_device_ids=true, to_apply=%region_17.0 | all-reduce | flops 1024 | bytes 8192 | tf_op jit(solution)/shard_map/pmax | solution.py:18
  514.1 4.4 exponential_reduce_fusion.5
  518.4 20.8 %psum.74 = f32[1024]{0:T(1024)S(1)} all-reduce(f32[1024]{0:T(1024)S(1)} %exponential_reduce_fusion.5), channel_id=1, replica_groups=mesh['src'=16,'tgt'=32] {'src'}, use_global_device_ids=true, to_apply=%region_19.0 | all-reduce | flops 1024 | bytes 8192 | tf_op jit(solution)/shard_map/psum | solution.py:19
  543.3 77.9 %pmax.67 = f32[2048]{0:T(1024)S(1)} all-reduce(f32[2048]{0:T(1024)S(1)} %subtract_reduce_fusion.4), channel_id=1, replica_groups=mesh['src'=16,'tgt'=32] {'tgt'}, use_global_device_ids=true, to_apply=%region_21.0 | all-reduce | flops 2048 | bytes 16384 | tf_op jit(solution)/shard_map/pmax | solution.py:12
  621.2 4.3 exponential_reduce_fusion.4
  625.5 63.7 %psum.75 = f32[2048]{0:T(1024)S(1)} all-reduce(f32[2048]{0:T(1024)S(1)} %exponential_reduce_fusion.4), channel_id=1, replica_groups=mesh['src'=16,'tgt'=32] {'tgt'}, use_global_device_ids=true, to_apply=%region_23.0 | all-reduce | flops 2048 | bytes 16384 | tf_op jit(solution)/shard_map/psum | solution.py:13
  693.2 21.0 %pmax.68 = f32[1024]{0:T(1024)S(1)} all-reduce(f32[1024]{0:T(1024)S(1)} %subtract_reduce_fusion.3), channel_id=1, replica_groups=mesh['src'=16,'tgt'=32] {'src'}, use_global_device_ids=true, to_apply=%region_25.0 | all-reduce | flops 1024 | bytes 8192 | tf_op jit(solution)/shard_map/pmax | solution.py:18
  714.3 4.4 exponential_reduce_fusion.3
  718.6 20.8 %psum.76 = f32[1024]{0:T(1024)S(1)} all-reduce(f32[1024]{0:T(1024)S(1)} %exponential_reduce_fusion.3), channel_id=1, replica_groups=mesh['src'=16,'tgt'=32] {'src'}, use_global_device_ids=true, to_apply=%region_27.0 | all-reduce | flops 1024 | bytes 8192 | tf_op jit(solution)/shard_map/psum | solution.py:19
  743.5 77.9 %pmax.69 = f32[2048]{0:T(1024)S(1)} all-reduce(f32[2048]{0:T(1024)S(1)} %subtract_reduce_fusion.2), channel_id=1, replica_groups=mesh['src'=16,'tgt'=32] {'tgt'}, use_global_device_ids=true, to_apply=%region_29.0 | all-reduce | flops 2048 | bytes 16384 | tf_op jit(solution)/shard_map/pmax | solution.py:12
  821.4 4.3 exponential_reduce_fusion.2
  825.7 63.7 %psum.77 = f32[2048]{0:T(1024)S(1)} all-reduce(f32[2048]{0:T(1024)S(1)} %exponential_reduce_fusion.2), channel_id=1, replica_groups=mesh['src'=16,'tgt'=32] {'tgt'}, use_global_device_ids=true, to_apply=%region_31.0 | all-reduce | flops 2048 | bytes 16384 | tf_op jit(solution)/shard_map/psum | solution.py:13
  893.4 21.0 %pmax.70 = f32[1024]{0:T(1024)S(1)} all-reduce(f32[1024]{0:T(1024)S(1)} %subtract_reduce_fusion.1), channel_id=1, replica_groups=mesh['src'=16,'tgt'=32] {'src'}, use_global_device_ids=true, to_apply=%region_33.0 | all-reduce | flops 1024 | bytes 8192 | tf_op jit(solution)/shard_map/pmax | solution.py:18
  914.5 4.4 exponential_reduce_fusion.1
  918.8 20.8 %psum.78 = f32[1024]{0:T(1024)S(1)} all-reduce(f32[1024]{0:T(1024)S(1)} %exponential_reduce_fusion.1), channel_id=1, replica_groups=mesh['src'=16,'tgt'=32] {'src'}, use_global_device_ids=true, to_apply=%region_35.0 | all-reduce | flops 1024 | bytes 8192 | tf_op jit(solution)/shard_map/psum | solution.py:19
  939.7 4.0 subtract_reduce_fusion
  943.7 77.9 %pmax.71 = f32[2048]{0:T(1024)S(1)} all-reduce(f32[2048]{0:T(1024)S(1)} %subtract_reduce_fusion), channel_id=1, replica_groups=mesh['src'=16,'tgt'=32] {'tgt'}, use_global_device_ids=true, to_apply=%region_37.0 | all-reduce | flops 2048 | bytes 16384 | tf_op jit(solution)/shard_map/pmax | solution.py:12
  1021.6 4.3 exponential_reduce_fusion
  1025.9 63.7 %psum.79 = f32[2048]{0:T(1024)S(1)} all-reduce(f32[2048]{0:T(1024)S(1)} %exponential_reduce_fusion), channel_id=1, replica_groups=mesh['src'=16,'tgt'=32] {'tgt'}, use_global_device_ids=true, to_apply=%region_39.0 | all-reduce | flops 2048 | bytes 16384 | tf_op jit(solution)/shard_map/psum | solution.py:13
  (22 shorter events, 30.0 us)
Async XLA Ops:
  889.4 200.2 %copy-start = (f32[2048]{0:T(1024)}, f32[2048]{0:T(1024)S(1)}, u32[]{:S(2)}) copy-start(f32[2048]{0:T(1024)S(1)} %add_subtract_fusion) | copy-start | bytes 24580
  939.7 86.3 %copy-start.1 = (f32[1024]{0:T(1024)}, f32[1024]{0:T(1024)S(1)}, u32[]{:S(2)}) copy-start(f32[1024]{0:T(1024)S(1)} %add_subtract_fusion.4) | copy-start | bytes 12292
where the time goes:
time: 1090 us
  blocking collectives  997 us (91%)
  other arithmetic  80.1 us (7%)
  matrix products  11.7 us (1%)
    pmax x5, blocking collectives, row_lse(): highest = lax.pmax(jnp.max(scores, 1), 'tgt')  375 us
    psum x5, blocking collectives, row_lse(): total = lax.psum(jnp.sum(jnp.exp(scores - highest[:, None]), 1), 'tgt')  320 us
    psum x1, blocking collectives, body(): mean_cost = lax.psum(jnp.sum(cost), ('src', 'tgt')) / (n_source * n_target)  105 us
    pmax x4, blocking collectives, col_lse(): highest = lax.pmax(jnp.max(scores, 0), 'src')  84.1 us
    psum x4, blocking collectives, col_lse(): total = lax.psum(jnp.sum(jnp.exp(scores - highest[None, :]), 0), 'src')  83.4 us
    all_gather x1, blocking collectives, body(): rows = lax.all_gather(source_latents, 'tgt', axis=0, tiled=True)  29.4 us
    reduce_max x5, other arithmetic, row_lse(): highest = lax.pmax(jnp.max(scores, 1), 'tgt')  22.6 us
    reduce_sum x5, other arithmetic, row_lse(): total = lax.psum(jnp.sum(jnp.exp(scores - highest[:, None]), 1), 'tgt')  22 us

commit v1 on v0

v1 whole, which is shorter than its diff:
```python
import functools
import math

import jax
import jax.numpy as jnp
from jax import lax
from jax.experimental import pallas as pl
from jax.experimental.pallas import tpu as pltpu
from jax.sharding import PartitionSpec as P

ITERS = 4
EDGE = 4
CHIPS = EDGE * EDGE
LAYERS = 16
WIDTH = 64
ROWS = 2048
COLS = 1024
ROW_TILES = ROWS // 128
COL_TILES = COLS // 128
DEPTH = 8 * WIDTH
CELLS = 32768
LOG_CELLS = math.log2(CELLS)
LIFT = 30.0
SCALE = 90.0
MESH = pl.DeviceIdType.MESH


def hops(step):
    return min(step, EDGE - step)


PLANE = sorted(
    ((dy, dx) for dy in range(EDGE) for dx in range(EDGE) if dy or dx),
    key=lambda step: -hops(step[0]) - hops(step[1]),
)
RING = sorted(range(1, LAYERS), key=lambda step: -min(step, LAYERS - step))


def split3(value):
    high = value.astype(jnp.bfloat16)
    rest = value - high.astype(jnp.float32)
    mid = rest.astype(jnp.bfloat16)
    low = (rest - mid.astype(jnp.float32)).astype(jnp.bfloat16)
    return high, mid, low


def kernel(
    x_hbm, yt_hbm, u_out, v_out, mass_out,
    x_in, x_pad, yt, ya, xt, tile, gx,
    stat_send, stat_slots, zstat_send, zstat_slots,
    row_send, row_sib, row_slots, col_send, col_slots,
    col_part, col_wide, row_max, row_norm, row_base, col_base, col_gain, alpha,
    in_sem, stat_sems, zstat_sems, gx_sems, fwd_sems,
    row_send_sem, row_sems, sib_send_sem, sib_sems, col_send_sem, col_sems,
):
    layer = lax.axis_index("src")
    place = lax.axis_index("tgt")
    core = lax.rem(place, 2)
    chip = place // 2
    px = lax.rem(chip, EDGE)
    py = chip // EDGE
    sibling = (layer, chip * 2 + 1 - core)

    def plane_chip(step):
        return lax.rem(py + step[0], EDGE) * EDGE + lax.rem(px + step[1], EDGE)

    plane_same = [(layer, plane_chip(step) * 2 + core) for step in PLANE]
    plane_other = [(layer, plane_chip(step) * 2 + 1 - core) for step in PLANE]
    ring = [(lax.rem(layer + step, LAYERS), place) for step in RING]

    def wait_bytes(ref, sem):
        pltpu.make_async_copy(ref, ref, sem).wait()

    def push(src, dst, send_sem, recv_sem, peer):
        pltpu.make_async_remote_copy(
            src_ref=src, dst_ref=dst, send_sem=send_sem, recv_sem=recv_sem,
            device_id=peer, device_id_type=MESH,
        ).start()

    x_pad[...] = jnp.zeros_like(x_pad)
    x_copy = pltpu.make_async_copy(x_hbm, x_in, in_sem.at[0])
    y_copy = pltpu.make_async_copy(yt_hbm, yt, in_sem.at[1])
    x_copy.start()
    y_copy.start()
    barrier = pltpu.get_barrier_semaphore()
    peers = ring + plane_same + plane_other + [sibling]
    for peer in peers:
        pl.semaphore_signal(barrier, inc=1, device_id=peer, device_id_type=MESH)
    x_copy.wait()
    y_copy.wait()
    x_pad[0:WIDTH, 0:WIDTH] = x_in[...]

    lanes = lax.broadcasted_iota(jnp.int32, (1, 128), 1)
    left = lanes < WIDTH

    x_wide = x_pad[...]
    x_turned = x_wide.T
    packed = x_turned[0:32, :] + pltpu.roll(x_turned[32:64, :], 64, 1)
    gx[core, chip] = packed

    y_sum = jnp.zeros((1, 128), jnp.float32)
    y_square = jnp.zeros((1, 128), jnp.float32)
    for block in range(COL_TILES):
        at = slice(block * 128, block * 128 + 128)
        piece = yt[:, at]
        wide = jnp.concatenate([piece, piece], 0).T
        square = wide * wide
        y_sum += jnp.sum(wide, 0, keepdims=True)
        y_square += jnp.sum(square, 0, keepdims=True)
        norm = jnp.sum(jnp.where(left, square, 0.0), 1, keepdims=True)
        high, mid, low = split3(wide)
        ya[at, 0:128] = high
        ya[at, 128:256] = mid
        ya[at, 256:384] = jnp.where(left, low.astype(jnp.float32), high.astype(jnp.float32)).astype(jnp.bfloat16)
        nh, nm, nl = split3(jnp.broadcast_to(norm, (128, 128)))
        tail = jnp.where(lanes == 0, nh.astype(jnp.float32), jnp.where(lanes == 1, nm.astype(jnp.float32), nl.astype(jnp.float32)))
        ya[at, 384:512] = jnp.where(lanes < 3, tail, 0.0).astype(jnp.bfloat16)
    x_sum = jnp.sum(x_wide, 0, keepdims=True)
    x_square = jnp.sum(x_wide * x_wide, 0, keepdims=True)
    stat_send[0:1, :] = jnp.where(left, x_sum, y_sum)
    stat_send[1:2, :] = jnp.where(left, x_square, y_square)
    stat_slots[place] = stat_send[...]

    pl.semaphore_wait(barrier, len(peers))

    for peer in plane_same + plane_other + [sibling]:
        push(stat_send, stat_slots.at[place], stat_sems.at[0], stat_sems.at[1], peer)
    for peer in plane_same:
        push(gx.at[core, chip], gx.at[core, chip], gx_sems.at[0], gx_sems.at[1], peer)
    wait_bytes(stat_slots.at[0 : 2 * CHIPS - 1], stat_sems.at[1])
    zstat_send[...] = jnp.sum(stat_slots[...], 0)
    zstat_slots[layer] = zstat_send[...]
    for peer in ring:
        push(zstat_send, zstat_slots.at[layer], zstat_sems.at[0], zstat_sems.at[1], peer)
    wait_bytes(gx.at[0, 0 : CHIPS - 1], gx_sems.at[1])
    push(gx.at[core], gx.at[core], fwd_sems.at[0], fwd_sems.at[1], sibling)
    wait_bytes(gx.at[0], fwd_sems.at[1])

    tail_row = lax.broadcasted_iota(jnp.int32, (128, 256), 0)
    tail_x = jnp.where(tail_row < 3, -1.0, 0.0).astype(jnp.bfloat16)

    def multiply(q, carry):
        halves = []
        for k in range(2):
            one = gx[0, 2 * q + k]
            two = gx[1, 2 * q + k]
            top = jnp.where(left, one, pltpu.roll(two, 64, 1))
            low = jnp.where(left, pltpu.roll(one, 64, 1), two)
            halves.append(jnp.concatenate([top, low], 0))
        full = jnp.concatenate(halves, 1)
        norm = jnp.sum(full * full, 0, keepdims=True)
        high, mid, low = split3(full * 2.0)
        xt[0:64, :] = high
        xt[64:128, :] = mid
        xt[128:192, :] = high
        xt[192:256, :] = mid
        xt[256:320, :] = high
        xt[320:384, :] = low
        xt[384:512, :] = tail_x
        product = jnp.dot(ya[...], xt[...], preferred_element_type=jnp.float32)
        at = pl.ds(pl.multiple_of(q * 256, 256), 256)
        tile[:, at] = product
        top = jnp.max(product, 0, keepdims=True)
        for k in range(2):
            row_max[pl.ds(2 * q + k, 1), :] = top[:, k * 128 : k * 128 + 128]
            row_norm[pl.ds(2 * q + k, 1), :] = norm[:, k * 128 : k * 128 + 128]
        return carry

    lax.fori_loop(0, ROWS // 256, multiply, 0)

    wait_bytes(zstat_slots.at[0 : LAYERS - 1], zstat_sems.at[1])
    total = jnp.sum(zstat_slots[...], 0) * jnp.where(left, 1.0 / CELLS, 1.0 / (CELLS * LAYERS))
    means = total[0:1, :]
    mean_cost = jnp.sum(total[1:2, :] - means * pltpu.roll(means, 64, 1), 1, keepdims=True)
    kappa = jnp.broadcast_to(math.log2(math.e) / (0.05 * mean_cost), (8, 128))

    def lane(t):
        return slice(t * 128, t * 128 + 128)

    def spread(ref, t):
        return jnp.broadcast_to(ref[t : t + 1, :], (8, 128))

    def row_exchange(parity, join):
        push(row_send, row_sib.at[parity], sib_send_sem, sib_sems.at[parity], sibling)
        wait_bytes(row_sib.at[parity], sib_sems.at[parity])
        wait_bytes(row_send, sib_send_sem)
        both = join(row_send[...], row_sib[parity])
        row_send[...] = both
        row_slots[parity, chip] = both
        for peer in plane_same:
            push(row_send, row_slots.at[parity, chip], row_send_sem, row_sems.at[parity], peer)
        wait_bytes(row_slots.at[parity, 0 : CHIPS - 1], row_sems.at[parity])
        wait_bytes(row_slots.at[parity, 0 : CHIPS - 1], row_send_sem)

    def col_exchange(parity):
        col_slots[parity, layer] = col_send[...]
        for peer in ring:
            push(col_send, col_slots.at[parity, layer], col_send_sem, col_sems.at[parity], peer)
        wait_bytes(col_slots.at[parity, 0 : LAYERS - 1], col_sems.at[parity])
        wait_bytes(col_slots.at[parity, 0 : LAYERS - 1], col_send_sem)

    def lse_pair(a, b):
        top = jnp.maximum(a, b)
        return top + jnp.log2(jnp.exp2(a - top) + jnp.exp2(b - top))

    def lse_slots(slots):
        top = jnp.max(slots, 0)
        return top + jnp.log2(jnp.sum(jnp.exp2(slots - top[None]), 0))

    def col_lanes(ref, pick):
        for block in range(COL_TILES):
            col_send[block : block + 1, :] = pick(ref[block * 128 : block * 128 + 128, :].T)

    def add_sublanes(block):
        return jnp.sum(block, 0, keepdims=True)

    row_max[...] = row_max[...] * kappa[0:1, :]
    GROUP = 4

    def first_rows(g, accs):
        accs = list(accs)
        for k in range(GROUP):
            at = pl.ds(pl.multiple_of(g * 8 * GROUP, 8) + 8 * k, 8)
            for t in range(ROW_TILES):
                accs[t] += jnp.exp2(tile[at, lane(t)] * kappa - spread(row_max, t))
        return tuple(accs)

    zeros = tuple(jnp.zeros((8, 128), jnp.float32) for _ in range(ROW_TILES))
    accs = lax.fori_loop(0, COLS // (8 * GROUP), first_rows, zeros)
    for t in range(ROW_TILES):
        row_send[t : t + 1, :] = row_max[t : t + 1, :] + jnp.log2(jnp.sum(accs[t], 0, keepdims=True))
    row_exchange(0, lse_pair)
    row_base[...] = -LOG_CELLS - lse_slots(row_slots[0])

    def first_max(g, carry):
        for k in range(GROUP):
            at = pl.ds(pl.multiple_of(g * 8 * GROUP, 8) + 8 * k, 8)
            top = tile[at, lane(0)] * kappa + spread(row_base, 0)
            for t in range(1, ROW_TILES):
                top = jnp.maximum(top, tile[at, lane(t)] * kappa + spread(row_base, t))
            col_part[at, :] = top
        return carry

    lax.fori_loop(0, COLS // (8 * GROUP), first_max, 0)
    for block in range(COL_TILES):
        at = slice(block * 128, block * 128 + 128)
        col_wide[at, :] = jnp.broadcast_to(jnp.max(col_part[at, :], 1, keepdims=True) - LIFT, (128, 128))

    def first_cols(g, carry):
        for k in range(GROUP):
            at = pl.ds(pl.multiple_of(g * 8 * GROUP, 8) + 8 * k, 8)
            top = col_wide[at, :]
            acc = None
            for t in range(ROW_TILES):
                power = jnp.exp2((tile[at, lane(t)] * kappa + spread(row_base, t)) - top)
                tile[at, lane(t)] = power
                acc = power if acc is None else acc + power
            col_part[at, :] = acc
        return carry

    lax.fori_loop(0, COLS // (8 * GROUP), first_cols, 0)
    col_lanes(col_wide, lambda block: block[0:1, :])
    col_gain[...] = col_send[...]
    col_lanes(col_part, add_sublanes)
    col_send[...] = col_gain[...] + jnp.log2(col_send[...])
    col_exchange(0)
    col_base[...] = -LOG_CELLS - lse_slots(col_slots[0])
    col_gain[...] = jnp.exp2(col_gain[...] + col_base[...] + SCALE)

    def spread_cols(value):
        turned = value.T
        for block in range(COL_TILES):
            col_wide[block * 128 : block * 128 + 128, :] = jnp.broadcast_to(turned[:, block : block + 1], (128, 128))

    def row_step(parity):
        def add_rows(g, accs):
            accs = list(accs)
            for k in range(GROUP):
                at = pl.ds(pl.multiple_of(g * 8 * GROUP, 8) + 8 * k, 8)
                gain = col_wide[at, :]
                for t in range(ROW_TILES):
                    accs[t] += tile[at, lane(t)] * gain
            return tuple(accs)

        accs = lax.fori_loop(0, COLS // (8 * GROUP), add_rows, zeros)
        for t in range(ROW_TILES):
            row_send[t : t + 1, :] = jnp.sum(accs[t], 0, keepdims=True)
        row_exchange(parity, jnp.add)
        return jnp.sum(row_slots[parity], 0)

    def col_step(parity):
        def add_cols(g, carry):
            for k in range(GROUP):
                at = pl.ds(pl.multiple_of(g * 8 * GROUP, 8) + 8 * k, 8)
                parts = [tile[at, lane(t)] * spread(alpha, t) for t in range(ROW_TILES)]
                while len(parts) > 1:
                    parts = [parts[i] + parts[i + 1] for i in range(0, len(parts), 2)]
                col_part[at, :] = parts[0]
            return carry

        lax.fori_loop(0, COLS // (8 * GROUP), add_cols, 0)
        col_lanes(col_part, add_sublanes)
        col_send[...] = col_send[...] * col_gain[...]
        col_exchange(parity)
        return jnp.sum(col_slots[parity], 0)

    ratio = 2.0 ** (SCALE - LOG_CELLS)
    spread_cols(col_gain[...])

    def iterate(step, carry):
        parity = lax.rem(step, 2)
        alpha[...] = ratio / row_step(parity)
        beta = ratio / col_step(parity)
        v_out[...] = (col_base[...] + jnp.log2(beta)) * math.log(2.0)
        spread_cols(beta * col_gain[...])
        return carry

    lax.fori_loop(1, ITERS, iterate, 0)
    u_out[...] = (row_base[...] + row_norm[...] * kappa[0:1, :] + jnp.log2(alpha[...])) * math.log(2.0)
    mass_out[...] = alpha[...] * (row_step(ITERS % 2) * (1.0 / ratio))
    wait_bytes(stat_slots.at[0 : 2 * CHIPS - 1], stat_sems.at[0])
    wait_bytes(zstat_slots.at[0 : LAYERS - 1], zstat_sems.at[0])
    wait_bytes(gx.at[0, 0 : CHIPS - 1], gx_sems.at[0])
    wait_bytes(gx.at[0], fwd_sems.at[0])


def body(source_latents, target_latents):
    f32, bf16 = jnp.float32, jnp.bfloat16
    vmem, dma = pltpu.VMEM, pltpu.SemaphoreType.DMA
    row, col = (ROW_TILES, 128), (COL_TILES, 128)
    any_space, in_vmem = pl.BlockSpec(memory_space=pl.ANY), pl.BlockSpec(memory_space=pltpu.VMEM)
    u, v, mass = pl.pallas_call(
        kernel,
        name="sinkhorn",
        out_shape=[jax.ShapeDtypeStruct(shape, f32) for shape in (row, col, row)],
        in_specs=[any_space, any_space],
        out_specs=[in_vmem] * 3,
        scratch_shapes=[
            vmem((WIDTH, WIDTH), f32),
            vmem((128, 128), f32),
            vmem((WIDTH, COLS), f32),
            vmem((COLS, DEPTH), bf16),
            vmem((DEPTH, 256), bf16),
            vmem((COLS, ROWS), f32),
            vmem((2, CHIPS, WIDTH // 2, 128), f32),
            vmem((2, 128), f32),
            vmem((2 * CHIPS, 2, 128), f32),
            vmem((2, 128), f32),
            vmem((LAYERS, 2, 128), f32),
            vmem(row, f32),
            vmem((2,) + row, f32),
            vmem((2, CHIPS) + row, f32),
            vmem(col, f32),
            vmem((2, LAYERS) + col, f32),
            vmem((COLS, 128), f32),
            vmem((COLS, 128), f32),
            vmem(row, f32),
            vmem(row, f32),
            vmem(row, f32),
            vmem(col, f32),
            vmem(col, f32),
            vmem(row, f32),
            dma((2,)),
            dma((2,)),
            dma((2,)),
            dma((2,)),
            dma((2,)),
            dma(()),
            dma((2,)),
            dma(()),
            dma((2,)),
            dma(()),
            dma((2,)),
        ],
        compiler_params=pltpu.CompilerParams(
            collective_id=0, has_side_effects=True, vmem_limit_bytes=40 * 1024 * 1024
        ),
    )(source_latents, target_latents.T)
    return u.reshape(ROWS), v.reshape(COLS), mass.reshape(ROWS)


def solution(mesh):
    in_specs = (P(("src", "tgt"), None), P("tgt", None))
    out_specs = (P("src"), P("tgt"), P("src"))
    return jax.shard_map(body, mesh=mesh, in_specs=in_specs, out_specs=out_specs, check_vma=False)
```

time: 1090 us -> 104 us (0.10)
  blocking collectives: 997 us -> 0 us
  Pallas kernels: 0 us -> 100 us
  other arithmetic: 80.1 us -> 0 us
  matrix products: 11.7 us -> 0 us
    psum x10 -> x0, blocking collectives: 508 us -> none  [the longest x5 320 us: row_lse(): total = lax.psum(jnp.sum(jnp.exp(scores - highest[:, None]), 1), 'tgt')]
    pmax x9 -> x0, blocking collectives: 459 us -> none  [the longest x5 375 us: row_lse(): highest = lax.pmax(jnp.max(scores, 1), 'tgt')]
    pallas_call x0 -> x1, Pallas kernels: none -> 100 us  [body(): pl.pallas_call(kernel, name='sinkhorn', out_shape=[jax.ShapeDtypeStruct(s...]
    reduce_sum x11 -> x0, other arithmetic: 40.8 us -> none  [the longest x5 22 us: row_lse(): total = lax.psum(jnp.sum(jnp.exp(scores - highest[:, None]), 1), 'tgt')]
    reduce_max x9 -> x0, other arithmetic: 38.6 us -> none  [the longest x5 22.6 us: row_lse(): highest = lax.pmax(jnp.max(scores, 1), 'tgt')]
    all_gather x1 -> x0, blocking collectives: 29.4 us -> none  [body(): rows = lax.all_gather(source_latents, 'tgt', axis=0, tiled=True)]
    dot_general x1 -> x0, matrix products: 11.7 us -> none  [body(): lax.dot_general(rows, target_latents, (((1,), (1,)), ((), ())), precision...]
where the time goes in v1:
time: 104 us
  Pallas kernels  100 us (96%)
  local copies, waits for them, and re-layouts  3.49 us (3%)
    pallas_call x1, Pallas kernels, body(): pl.pallas_call(kernel, name='sinkhorn', out_shape=[jax.ShapeDtypeStruct(s...  100 us
    unnamed x7, local copies, waits for them, and re-layouts  3.49 us

profile of v1, /device:TPU:1, one launch (start us, length us, event | category | flops | bytes accessed | tf_op | source)
XLA Modules:
  0.0 104.1 jit_solution(9535385407715059538)
XLA Ops:
  0.6 0.0 copy-start
  0.6 0.9 copy-done
  1.6 0.0 copy-start.1
  1.6 0.8 copy-done.1
  2.3 100.0 %sinkhorn.1 = (f32[16,128]{1,0:T(8,128)S(1)}, f32[8,128]{1,0:T(8,128)S(1)}, f32[16,128]{1,0:T(8,128)S(1)}) custom-call(f32[64,64]{1,0:T(8,128)S(1)} %copy-done.1, f32[64,1024]{1,0:T(8,128)S(1)} %bitcast.4), custom_call_target="tpu_custom_call" | custom-call | tf_op jit(solution)/shard_map/sinkhorn/pallas_call | solution.py:332
  102.3 0.6 copy.8
  102.9 0.6 copy.9
  103.5 0.6 copy.10
Async XLA Ops:
  0.6 1.0 copy-start
  1.6 0.8 copy-start.1

commit v2 on v1

--- a/solution.py
+++ b/solution.py
@@ -45,12 +45,12 @@
 
 
 def kernel(
-    x_hbm, yt_hbm, u_out, v_out, mass_out,
-    x_in, x_pad, yt, ya, xt, tile, gx,
+    x_hbm, yt_hbm, u_out, v_out,
+    x_in, x_pad, yt, ya, xt, tile, powers, gx,
     stat_send, stat_slots, zstat_send, zstat_slots,
     row_send, row_sib, row_slots, col_send, col_slots,
-    col_part, col_wide, row_max, row_norm, row_base, col_base, col_gain, alpha,
-    in_sem, stat_sems, zstat_sems, gx_sems, fwd_sems,
+    col_part, col_wide, row_max, row_norm, row_base, row_shift, col_base, col_gain, alpha,
+    ring_sem, in_sem, stat_sems, zstat_sems, gx_send_sem, gx_sems, fwd_send_sem, fwd_sems,
     row_send_sem, row_sems, sib_send_sem, sib_sems, col_send_sem, col_sems,
 ):
     layer = lax.axis_index("src")
@@ -77,17 +77,17 @@
             device_id=peer, device_id_type=MESH,
         ).start()
 
-    x_pad[...] = jnp.zeros_like(x_pad)
+    barrier = pltpu.get_barrier_semaphore()
+    near = [(lax.rem(layer + step, LAYERS), place) for step in range(1, LAYERS) if min(step, LAYERS - step) <= LAYERS // 4]
+    peers = plane_same + plane_other + [sibling] + near
+    for peer in peers:
+        pl.semaphore_signal(barrier, inc=1, device_id=peer, device_id_type=MESH)
     x_copy = pltpu.make_async_copy(x_hbm, x_in, in_sem.at[0])
     y_copy = pltpu.make_async_copy(yt_hbm, yt, in_sem.at[1])
     x_copy.start()
     y_copy.start()
-    barrier = pltpu.get_barrier_semaphore()
-    peers = ring + plane_same + plane_other + [sibling]
-    for peer in peers:
-        pl.semaphore_signal(barrier, inc=1, device_id=peer, device_id_type=MESH)
+    x_pad[...] = jnp.zeros_like(x_pad)
     x_copy.wait()
-    y_copy.wait()
     x_pad[0:WIDTH, 0:WIDTH] = x_in[...]
 
     lanes = lax.broadcasted_iota(jnp.int32, (1, 128), 1)
@@ -95,19 +95,43 @@
 
     x_wide = x_pad[...]
     x_turned = x_wide.T
-    packed = x_turned[0:32, :] + pltpu.roll(x_turned[32:64, :], 64, 1)
-    gx[core, chip] = packed
+    gx[core, chip] = x_turned[0:32, :] + pltpu.roll(x_turned[32:64, :], 64, 1)
+    x_sum = jnp.sum(x_wide, 0, keepdims=True)
+    x_square = jnp.sum(x_wide * x_wide, 0, keepdims=True)
 
     y_sum = jnp.zeros((1, 128), jnp.float32)
     y_square = jnp.zeros((1, 128), jnp.float32)
+    y_copy.wait()
     for block in range(COL_TILES):
         at = slice(block * 128, block * 128 + 128)
         piece = yt[:, at]
         wide = jnp.concatenate([piece, piece], 0).T
-        square = wide * wide
+        col_wide[at, :] = wide
         y_sum += jnp.sum(wide, 0, keepdims=True)
-        y_square += jnp.sum(square, 0, keepdims=True)
-        norm = jnp.sum(jnp.where(left, square, 0.0), 1, keepdims=True)
+        y_square += jnp.sum(wide * wide, 0, keepdims=True)
+    stat_send[0:1, :] = jnp.where(left, x_sum, y_sum)
+    stat_send[1:2, :] = jnp.where(left, x_square, y_square)
+    stat_slots[place] = stat_send[...]
+
+    pl.semaphore_wait(barrier, len(peers))
+    for step in (LAYERS // 4, LAYERS - LAYERS // 4):
+        peer = (lax.rem(layer + step, LAYERS), place)
+        pl.semaphore_signal(ring_sem, inc=1, device_id=peer, device_id_type=MESH)
+
+    for peer in plane_same + plane_other + [sibling]:
+        push(stat_send, stat_slots.at[place], stat_sems.at[0], stat_sems.at[1], peer)
+    for peer in plane_same[::-1]:
+        push(gx.at[core, chip], gx.at[core, chip], gx_send_sem, gx_sems.at[chip], peer)
+
+    def forward(at):
+        push(gx.at[core, at], gx.at[core, at], fwd_send_sem, fwd_sems.at[at], sibling)
+
+    forward(chip)
+
+    for block in range(COL_TILES):
+        at = slice(block * 128, block * 128 + 128)
+        wide = col_wide[at, :]
+        norm = jnp.sum(jnp.where(left, wide * wide, 0.0), 1, keepdims=True)
         high, mid, low = split3(wide)
         ya[at, 0:128] = high
         ya[at, 128:256] = mid
@@ -115,32 +139,30 @@
         nh, nm, nl = split3(jnp.broadcast_to(norm, (128, 128)))
         tail = jnp.where(lanes == 0, nh.astype(jnp.float32), jnp.where(lanes == 1, nm.astype(jnp.float32), nl.astype(jnp.float32)))
         ya[at, 384:512] = jnp.where(lanes < 3, tail, 0.0).astype(jnp.bfloat16)
-    x_sum = jnp.sum(x_wide, 0, keepdims=True)
-    x_square = jnp.sum(x_wide * x_wide, 0, keepdims=True)
-    stat_send[0:1, :] = jnp.where(left, x_sum, y_sum)
-    stat_send[1:2, :] = jnp.where(left, x_square, y_square)
-    stat_slots[place] = stat_send[...]
-
-    pl.semaphore_wait(barrier, len(peers))
-
-    for peer in plane_same + plane_other + [sibling]:
-        push(stat_send, stat_slots.at[place], stat_sems.at[0], stat_sems.at[1], peer)
-    for peer in plane_same:
-        push(gx.at[core, chip], gx.at[core, chip], gx_sems.at[0], gx_sems.at[1], peer)
+    tail_row = lax.broadcasted_iota(jnp.int32, (128, 256), 0)
+    xt[384:512, :] = jnp.where(tail_row < 3, -1.0, 0.0).astype(jnp.bfloat16)
+
     wait_bytes(stat_slots.at[0 : 2 * CHIPS - 1], stat_sems.at[1])
     zstat_send[...] = jnp.sum(stat_slots[...], 0)
     zstat_slots[layer] = zstat_send[...]
+    pl.semaphore_wait(ring_sem, 2)
     for peer in ring:
         push(zstat_send, zstat_slots.at[layer], zstat_sems.at[0], zstat_sems.at[1], peer)
-    wait_bytes(gx.at[0, 0 : CHIPS - 1], gx_sems.at[1])
-    push(gx.at[core], gx.at[core], fwd_sems.at[0], fwd_sems.at[1], sibling)
-    wait_bytes(gx.at[0], fwd_sems.at[1])
-
-    tail_row = lax.broadcasted_iota(jnp.int32, (128, 256), 0)
-    tail_x = jnp.where(tail_row < 3, -1.0, 0.0).astype(jnp.bfloat16)
-
-    def multiply(q, carry):
+
+    def pair(step):
+        turn = step // 2
+        dy = turn + (turn // 2) * (1 - 2 * lax.rem(turn, 2))
+        dx = lax.rem(step, 2)
+        return lax.rem(py + dy, EDGE) * 2 + lax.rem(px // 2 + dx, 2)
+
+    def receive(at):
+        wait_bytes(gx.at[0, 0], gx_sems.at[at])
+        forward(at)
+
+    def multiply(q):
         halves = []
+        for k in range(2):
+            wait_bytes(gx.at[0, 0], fwd_sems.at[2 * q + k])
         for k in range(2):
             one = gx[0, 2 * q + k]
             two = gx[1, 2 * q + k]
@@ -156,17 +178,23 @@
         xt[192:256, :] = mid
         xt[256:320, :] = high
         xt[320:384, :] = low
-        xt[384:512, :] = tail_x
         product = jnp.dot(ya[...], xt[...], preferred_element_type=jnp.float32)
-        at = pl.ds(pl.multiple_of(q * 256, 256), 256)
-        tile[:, at] = product
+        tile[:, pl.ds(pl.multiple_of(q * 256, 256), 256)] = product
         top = jnp.max(product, 0, keepdims=True)
         for k in range(2):
             row_max[pl.ds(2 * q + k, 1), :] = top[:, k * 128 : k * 128 + 128]
             row_norm[pl.ds(2 * q + k, 1), :] = norm[:, k * 128 : k * 128 + 128]
+
+    def stage(step, carry):
+        ahead = pair(step)
+        receive(2 * ahead)
+        receive(2 * ahead + 1)
+        multiply(pair(step - 1))
         return carry
 
-    lax.fori_loop(0, ROWS // 256, multiply, 0)
+    receive(chip + 1 - 2 * lax.rem(px, 2))
+    lax.fori_loop(1, CHIPS // 2, stage, 0)
+    multiply(pair(CHIPS // 2 - 1))
 
     wait_bytes(zstat_slots.at[0 : LAYERS - 1], zstat_sems.at[1])
     total = jnp.sum(zstat_slots[...], 0) * jnp.where(left, 1.0 / CELLS, 1.0 / (CELLS * LAYERS))
@@ -215,14 +243,16 @@
         return jnp.sum(block, 0, keepdims=True)
 
     row_max[...] = row_max[...] * kappa[0:1, :]
-    GROUP = 4
+    GROUP = 8
+
+    tops = [spread(row_max, t) for t in range(ROW_TILES)]
 
     def first_rows(g, accs):
         accs = list(accs)
         for k in range(GROUP):
             at = pl.ds(pl.multiple_of(g * 8 * GROUP, 8) + 8 * k, 8)
             for t in range(ROW_TILES):
-                accs[t] += jnp.exp2(tile[at, lane(t)] * kappa - spread(row_max, t))
+                accs[t] += jnp.exp2(tile[at, lane(t)] * kappa - tops[t])
         return tuple(accs)
 
     zeros = tuple(jnp.zeros((8, 128), jnp.float32) for _ in range(ROW_TILES))
@@ -232,35 +262,41 @@
     row_exchange(0, lse_pair)
     row_base[...] = -LOG_CELLS - lse_slots(row_slots[0])
 
+    row_shift[...] = row_base[...] / kappa[0:1, :]
+    shifts = [spread(row_shift, t) for t in range(ROW_TILES)]
+
+    def tree(parts, join):
+        while len(parts) > 1:
+            parts = [join(parts[i], parts[i + 1]) for i in range(0, len(parts), 2)]
+        return parts[0]
+
     def first_max(g, carry):
         for k in range(GROUP):
             at = pl.ds(pl.multiple_of(g * 8 * GROUP, 8) + 8 * k, 8)
-            top = tile[at, lane(0)] * kappa + spread(row_base, 0)
-            for t in range(1, ROW_TILES):
-                top = jnp.maximum(top, tile[at, lane(t)] * kappa + spread(row_base, t))
-            col_part[at, :] = top
+            col_part[at, :] = tree([tile[at, lane(t)] + shifts[t] for t in range(ROW_TILES)], jnp.maximum)
         return carry
 
     lax.fori_loop(0, COLS // (8 * GROUP), first_max, 0)
+    lift = LIFT / kappa[0:1, :]
     for block in range(COL_TILES):
         at = slice(block * 128, block * 128 + 128)
-        col_wide[at, :] = jnp.broadcast_to(jnp.max(col_part[at, :], 1, keepdims=True) - LIFT, (128, 128))
+        col_wide[at, :] = jnp.broadcast_to(jnp.max(col_part[at, :], 1, keepdims=True) - lift, (128, 128))
 
     def first_cols(g, carry):
         for k in range(GROUP):
             at = pl.ds(pl.multiple_of(g * 8 * GROUP, 8) + 8 * k, 8)
             top = col_wide[at, :]
-            acc = None
+            parts = []
             for t in range(ROW_TILES):
-                power = jnp.exp2((tile[at, lane(t)] * kappa + spread(row_base, t)) - top)
-                tile[at, lane(t)] = power
-                acc = power if acc is None else acc + power
-            col_part[at, :] = acc
+                power = jnp.exp2((tile[at, lane(t)] + shifts[t] - top) * kappa)
+                powers[at, lane(t)] = power
+                parts.append(power)
+            col_part[at, :] = tree(parts, jnp.add)
         return carry
 
     lax.fori_loop(0, COLS // (8 * GROUP), first_cols, 0)
     col_lanes(col_wide, lambda block: block[0:1, :])
-    col_gain[...] = col_send[...]
+    col_gain[...] = col_send[...] * kappa
     col_lanes(col_part, add_sublanes)
     col_send[...] = col_gain[...] + jnp.log2(col_send[...])
     col_exchange(0)
@@ -279,7 +315,7 @@
                 at = pl.ds(pl.multiple_of(g * 8 * GROUP, 8) + 8 * k, 8)
                 gain = col_wide[at, :]
                 for t in range(ROW_TILES):
-                    accs[t] += tile[at, lane(t)] * gain
+                    accs[t] += powers[at, lane(t)] * gain
             return tuple(accs)
 
         accs = lax.fori_loop(0, COLS // (8 * GROUP), add_rows, zeros)
@@ -289,13 +325,12 @@
         return jnp.sum(row_slots[parity], 0)
 
     def col_step(parity):
+        alphas = [spread(alpha, t) for t in range(ROW_TILES)]
+
         def add_cols(g, carry):
             for k in range(GROUP):
                 at = pl.ds(pl.multiple_of(g * 8 * GROUP, 8) + 8 * k, 8)
-                parts = [tile[at, lane(t)] * spread(alpha, t) for t in range(ROW_TILES)]
-                while len(parts) > 1:
-                    parts = [parts[i] + parts[i + 1] for i in range(0, len(parts), 2)]
-                col_part[at, :] = parts[0]
+                col_part[at, :] = tree([powers[at, lane(t)] * alphas[t] for t in range(ROW_TILES)], jnp.add)
             return carry
 
         lax.fori_loop(0, COLS // (8 * GROUP), add_cols, 0)
@@ -316,25 +351,26 @@
         return carry
 
     lax.fori_loop(1, ITERS, iterate, 0)
-    u_out[...] = (row_base[...] + row_norm[...] * kappa[0:1, :] + jnp.log2(alpha[...])) * math.log(2.0)
-    mass_out[...] = alpha[...] * (row_step(ITERS % 2) * (1.0 / ratio))
+    u_out[0] = alpha[...]
+    u_out[1] = row_base[...] + row_norm[...] * kappa[0:1, :]
+    u_out[2] = row_step(ITERS % 2) * (1.0 / ratio)
     wait_bytes(stat_slots.at[0 : 2 * CHIPS - 1], stat_sems.at[0])
     wait_bytes(zstat_slots.at[0 : LAYERS - 1], zstat_sems.at[0])
-    wait_bytes(gx.at[0, 0 : CHIPS - 1], gx_sems.at[0])
-    wait_bytes(gx.at[0], fwd_sems.at[0])
+    wait_bytes(gx.at[0, 0 : CHIPS - 1], gx_send_sem)
+    wait_bytes(gx.at[0], fwd_send_sem)
 
 
 def body(source_latents, target_latents):
     f32, bf16 = jnp.float32, jnp.bfloat16
     vmem, dma = pltpu.VMEM, pltpu.SemaphoreType.DMA
     row, col = (ROW_TILES, 128), (COL_TILES, 128)
-    any_space, in_vmem = pl.BlockSpec(memory_space=pl.ANY), pl.BlockSpec(memory_space=pltpu.VMEM)
-    u, v, mass = pl.pallas_call(
+    in_hbm, in_vmem = pl.BlockSpec(memory_space=pltpu.HBM), pl.BlockSpec(memory_space=pltpu.VMEM)
+    rows, v = pl.pallas_call(
         kernel,
         name="sinkhorn",
-        out_shape=[jax.ShapeDtypeStruct(shape, f32) for shape in (row, col, row)],
-        in_specs=[any_space, any_space],
-        out_specs=[in_vmem] * 3,
+        out_shape=[jax.ShapeDtypeStruct(shape, f32) for shape in ((3,) + row, col)],
+        in_specs=[in_hbm, in_hbm],
+        out_specs=[in_vmem] * 2,
         scratch_shapes=[
             vmem((WIDTH, WIDTH), f32),
             vmem((128, 128), f32),
@@ -342,6 +378,7 @@
             vmem((COLS, DEPTH), bf16),
             vmem((DEPTH, 256), bf16),
             vmem((COLS, ROWS), f32),
+            vmem((COLS, ROWS), f32),
             vmem((2, CHIPS, WIDTH // 2, 128), f32),
             vmem((2, 128), f32),
             vmem((2 * CHIPS, 2, 128), f32),
@@ -357,14 +394,18 @@
             vmem(row, f32),
             vmem(row, f32),
             vmem(row, f32),
+            vmem(row, f32),
             vmem(col, f32),
             vmem(col, f32),
             vmem(row, f32),
-            dma((2,)),
-            dma((2,)),
-            dma((2,)),
-            dma((2,)),
-            dma((2,)),
+            pltpu.SemaphoreType.REGULAR,
+            dma((2,)),
+            dma((2,)),
+            dma((2,)),
+            dma(()),
+            dma((CHIPS,)),
+            dma(()),
+            dma((CHIPS,)),
             dma(()),
             dma((2,)),
             dma(()),
@@ -375,8 +416,13 @@
         compiler_params=pltpu.CompilerParams(
             collective_id=0, has_side_effects=True, vmem_limit_bytes=40 * 1024 * 1024
         ),
-    )(source_latents, target_latents.T)
-    return u.reshape(ROWS), v.reshape(COLS), mass.reshape(ROWS)
+    )(
+        pltpu.with_memory_space_constraint(source_latents, pltpu.HBM),
+        pltpu.with_memory_space_constraint(target_latents.T, pltpu.HBM),
+    )
+    factor, first, mass = rows[0], rows[1], rows[2]
+    u = (first + jnp.log2(factor)) * math.log(2.0)
+    return u.reshape(ROWS), v.reshape(COLS), (factor * mass).reshape(ROWS)
 
 
 def solution(mesh):

time: 104 us -> 97.8 us (0.940)
  Pallas kernels: 100 us -> 95.8 us
  local copies, waits for them, and re-layouts: 3.49 us -> 0.59 us
    pallas_call x1, Pallas kernels: 100 us -> 95.8 us  [body(): pl.pallas_call(kernel, name='sinkhorn', out_shape=[jax.ShapeDtypeStruct(s...]
    unnamed x7 -> x1, local copies, waits for them, and re-layouts: 3.49 us -> 0.59 us
where the time goes in v2:
time: 97.8 us; the launch traced here: 97.6 us
  Pallas kernels  95.8 us (98%)
    pallas_call x1, Pallas kernels, body(): pl.pallas_call(kernel, name='sinkhorn', out_shape=[jax.ShapeDtypeStruct(s...  95.8 us

profile of v2, /device:TPU:1, one launch (start us, length us, event | category | flops | bytes accessed | tf_op | source)
XLA Modules:
  0.0 97.6 jit_solution(12903483246093366710)
XLA Ops:
  0.6 95.8 %sinkhorn.1 = (f32[3,16,128]{2,1,0:T(8,128)S(1)}, f32[8,128]{1,0:T(8,128)S(1)}) custom-call(f32[64,64]{1,0:T(8,128)} %x_hbm.1, f32[64,1024]{1,0:T(8,128)} %bitcast.7), custom_call_target="tpu_custom_call" | custom-call | tf_op jit(solution)/shard_map/sinkhorn/pallas_call | solution.py:368
  96.4 0.6 multiply_bitcast_fusion
  97.1 0.6 copy.6

commit v3 on v2

--- a/solution.py
+++ b/solution.py
@@ -22,6 +22,7 @@
 LOG_CELLS = math.log2(CELLS)
 LIFT = 30.0
 SCALE = 90.0
+FAR_HOPS = 9
 MESH = pl.DeviceIdType.MESH
 
 
@@ -33,6 +34,7 @@
     ((dy, dx) for dy in range(EDGE) for dx in range(EDGE) if dy or dx),
     key=lambda step: -hops(step[0]) - hops(step[1]),
 )
+FAR = [step for step in PLANE if hops(step[0]) + hops(step[1]) >= FAR_HOPS]
 RING = sorted(range(1, LAYERS), key=lambda step: -min(step, LAYERS - step))
 
 
@@ -48,8 +50,8 @@
     x_hbm, yt_hbm, u_out, v_out,
     x_in, x_pad, yt, ya, xt, tile, powers, gx,
     stat_send, stat_slots, zstat_send, zstat_slots,
-    row_send, row_sib, row_slots, col_send, col_slots,
-    col_part, col_wide, row_max, row_norm, row_base, row_shift, col_base, col_gain, alpha,
+    row_send, row_both, row_sib, row_slots, col_send, col_slots,
+    col_part, col_wide, row_max, row_norm, row_base, row_shift, col_base, col_gain, alpha, beta,
     ring_sem, in_sem, stat_sems, zstat_sems, gx_send_sem, gx_sems, fwd_send_sem, fwd_sems,
     row_send_sem, row_sems, sib_send_sem, sib_sems, col_send_sem, col_sems,
 ):
@@ -66,6 +68,7 @@
 
     plane_same = [(layer, plane_chip(step) * 2 + core) for step in PLANE]
     plane_other = [(layer, plane_chip(step) * 2 + 1 - core) for step in PLANE]
+    plane_both = [peer for both in zip(plane_same, plane_other) for peer in both] + [sibling]
     ring = [(lax.rem(layer + step, LAYERS), place) for step in RING]
 
     def wait_bytes(ref, sem):
@@ -77,15 +80,15 @@
             device_id=peer, device_id_type=MESH,
         ).start()
 
-    barrier = pltpu.get_barrier_semaphore()
-    near = [(lax.rem(layer + step, LAYERS), place) for step in range(1, LAYERS) if min(step, LAYERS - step) <= LAYERS // 4]
-    peers = plane_same + plane_other + [sibling] + near
-    for peer in peers:
-        pl.semaphore_signal(barrier, inc=1, device_id=peer, device_id_type=MESH)
     x_copy = pltpu.make_async_copy(x_hbm, x_in, in_sem.at[0])
     y_copy = pltpu.make_async_copy(yt_hbm, yt, in_sem.at[1])
     x_copy.start()
     y_copy.start()
+    barrier = pltpu.get_barrier_semaphore()
+    near = [(lax.rem(layer + step, LAYERS), place) for step in RING if min(step, LAYERS - step) <= LAYERS // 4]
+    peers = near[:2] + plane_both + near[2:]
+    for peer in peers:
+        pl.semaphore_signal(barrier, inc=1, device_id=peer, device_id_type=MESH)
     x_pad[...] = jnp.zeros_like(x_pad)
     x_copy.wait()
     x_pad[0:WIDTH, 0:WIDTH] = x_in[...]
@@ -118,7 +121,7 @@
         peer = (lax.rem(layer + step, LAYERS), place)
         pl.semaphore_signal(ring_sem, inc=1, device_id=peer, device_id_type=MESH)
 
-    for peer in plane_same + plane_other + [sibling]:
+    for peer in plane_both:
         push(stat_send, stat_slots.at[place], stat_sems.at[0], stat_sems.at[1], peer)
     for peer in plane_same[::-1]:
         push(gx.at[core, chip], gx.at[core, chip], gx_send_sem, gx_sems.at[chip], peer)
@@ -209,16 +212,25 @@
         return jnp.broadcast_to(ref[t : t + 1, :], (8, 128))
 
     def row_exchange(parity, join):
+        arrived = row_sems.at[parity]
         push(row_send, row_sib.at[parity], sib_send_sem, sib_sems.at[parity], sibling)
+        for step, same, other in zip(PLANE, plane_same, plane_other):
+            if step in FAR:
+                back = FAR.index(((EDGE - step[0]) % EDGE, (EDGE - step[1]) % EDGE))
+                push(row_send, row_slots.at[parity, chip], row_send_sem, arrived, same)
+                push(row_send, row_slots.at[parity, CHIPS + back], row_send_sem, arrived, other)
         wait_bytes(row_sib.at[parity], sib_sems.at[parity])
+        row_both[...] = join(row_send[...], row_sib[parity])
+        for step, same in zip(PLANE, plane_same):
+            if step not in FAR:
+                push(row_both, row_slots.at[parity, chip], row_send_sem, arrived, same)
+        row_slots[parity, chip] = row_both[...]
+        wait_bytes(row_slots.at[parity, 0 : CHIPS - 1 + len(FAR)], arrived)
+        for k, step in enumerate(FAR):
+            at = plane_chip(step)
+            row_slots[parity, at] = join(row_slots[parity, at], row_slots[parity, CHIPS + k])
         wait_bytes(row_send, sib_send_sem)
-        both = join(row_send[...], row_sib[parity])
-        row_send[...] = both
-        row_slots[parity, chip] = both
-        for peer in plane_same:
-            push(row_send, row_slots.at[parity, chip], row_send_sem, row_sems.at[parity], peer)
-        wait_bytes(row_slots.at[parity, 0 : CHIPS - 1], row_sems.at[parity])
-        wait_bytes(row_slots.at[parity, 0 : CHIPS - 1], row_send_sem)
+        wait_bytes(row_slots.at[parity, 0 : CHIPS - 1 + len(FAR)], row_send_sem)
 
     def col_exchange(parity):
         col_slots[parity, layer] = col_send[...]
@@ -243,7 +255,7 @@
         return jnp.sum(block, 0, keepdims=True)
 
     row_max[...] = row_max[...] * kappa[0:1, :]
-    GROUP = 8
+    GROUP = 16
 
     tops = [spread(row_max, t) for t in range(ROW_TILES)]
 
@@ -260,7 +272,7 @@
     for t in range(ROW_TILES):
         row_send[t : t + 1, :] = row_max[t : t + 1, :] + jnp.log2(jnp.sum(accs[t], 0, keepdims=True))
     row_exchange(0, lse_pair)
-    row_base[...] = -LOG_CELLS - lse_slots(row_slots[0])
+    row_base[...] = -LOG_CELLS - lse_slots(row_slots[0, 0:CHIPS])
 
     row_shift[...] = row_base[...] / kappa[0:1, :]
     shifts = [spread(row_shift, t) for t in range(ROW_TILES)]
@@ -303,57 +315,45 @@
     col_base[...] = -LOG_CELLS - lse_slots(col_slots[0])
     col_gain[...] = jnp.exp2(col_gain[...] + col_base[...] + SCALE)
 
-    def spread_cols(value):
-        turned = value.T
+    def row_step(parity, gains):
+        turned = gains.T
+        accs = list(zeros)
         for block in range(COL_TILES):
-            col_wide[block * 128 : block * 128 + 128, :] = jnp.broadcast_to(turned[:, block : block + 1], (128, 128))
-
-    def row_step(parity):
-        def add_rows(g, accs):
-            accs = list(accs)
-            for k in range(GROUP):
-                at = pl.ds(pl.multiple_of(g * 8 * GROUP, 8) + 8 * k, 8)
-                gain = col_wide[at, :]
+            for k in range(16):
+                gain = jnp.broadcast_to(turned[8 * k : 8 * k + 8, block : block + 1], (8, 128))
+                at = slice(128 * block + 8 * k, 128 * block + 8 * k + 8)
                 for t in range(ROW_TILES):
                     accs[t] += powers[at, lane(t)] * gain
-            return tuple(accs)
-
-        accs = lax.fori_loop(0, COLS // (8 * GROUP), add_rows, zeros)
         for t in range(ROW_TILES):
             row_send[t : t + 1, :] = jnp.sum(accs[t], 0, keepdims=True)
         row_exchange(parity, jnp.add)
-        return jnp.sum(row_slots[parity], 0)
+        return jnp.sum(row_slots[parity, 0:CHIPS], 0)
 
     def col_step(parity):
         alphas = [spread(alpha, t) for t in range(ROW_TILES)]
-
-        def add_cols(g, carry):
-            for k in range(GROUP):
-                at = pl.ds(pl.multiple_of(g * 8 * GROUP, 8) + 8 * k, 8)
-                col_part[at, :] = tree([powers[at, lane(t)] * alphas[t] for t in range(ROW_TILES)], jnp.add)
-            return carry
-
-        lax.fori_loop(0, COLS // (8 * GROUP), add_cols, 0)
-        col_lanes(col_part, add_sublanes)
-        col_send[...] = col_send[...] * col_gain[...]
+        for block in range(COL_TILES):
+            parts = []
+            for k in range(16):
+                at = slice(128 * block + 8 * k, 128 * block + 8 * k + 8)
+                parts.append(tree([powers[at, lane(t)] * alphas[t] for t in range(ROW_TILES)], jnp.add))
+            total = jnp.sum(jnp.concatenate(parts, 0).T, 0, keepdims=True)
+            col_send[block : block + 1, :] = total * col_gain[block : block + 1, :]
         col_exchange(parity)
         return jnp.sum(col_slots[parity], 0)
 
     ratio = 2.0 ** (SCALE - LOG_CELLS)
-    spread_cols(col_gain[...])
-
-    def iterate(step, carry):
+
+    def iterate(step, gains):
         parity = lax.rem(step, 2)
-        alpha[...] = ratio / row_step(parity)
-        beta = ratio / col_step(parity)
-        v_out[...] = (col_base[...] + jnp.log2(beta)) * math.log(2.0)
-        spread_cols(beta * col_gain[...])
-        return carry
-
-    lax.fori_loop(1, ITERS, iterate, 0)
+        alpha[...] = ratio / row_step(parity, gains)
+        beta[...] = ratio / col_step(parity)
+        return beta[...] * col_gain[...]
+
+    u_out[1] = row_base[...] + row_norm[...] * kappa[0:1, :]
+    gains = lax.fori_loop(1, ITERS, iterate, col_gain[...])
     u_out[0] = alpha[...]
-    u_out[1] = row_base[...] + row_norm[...] * kappa[0:1, :]
-    u_out[2] = row_step(ITERS % 2) * (1.0 / ratio)
+    v_out[...] = (col_base[...] + jnp.log2(beta[...])) * math.log(2.0)
+    u_out[2] = row_step(ITERS % 2, gains) * (1.0 / ratio)
     wait_bytes(stat_slots.at[0 : 2 * CHIPS - 1], stat_sems.at[0])
     wait_bytes(zstat_slots.at[0 : LAYERS - 1], zstat_sems.at[0])
     wait_bytes(gx.at[0, 0 : CHIPS - 1], gx_send_sem)
@@ -385,8 +385,9 @@
             vmem((2, 128), f32),
             vmem((LAYERS, 2, 128), f32),
             vmem(row, f32),
+            vmem(row, f32),
             vmem((2,) + row, f32),
-            vmem((2, CHIPS) + row, f32),
+            vmem((2, CHIPS + len(FAR)) + row, f32),
             vmem(col, f32),
             vmem((2, LAYERS) + col, f32),
             vmem((COLS, 128), f32),
@@ -398,6 +399,7 @@
             vmem(col, f32),
             vmem(col, f32),
             vmem(row, f32),
+            vmem(col, f32),
             pltpu.SemaphoreType.REGULAR,
             dma((2,)),
             dma((2,)),

time: 97.8 us -> 93.9 us (0.960)
  Pallas kernels: 95.8 us -> 91.9 us
    pallas_call x1, Pallas kernels: 95.8 us -> 91.9 us  [body(): pl.pallas_call(kernel, name='sinkhorn', out_shape=[jax.ShapeDtypeStruct(s...]
where the time goes in v3:
time: 93.9 us; the launch traced here: 93.7 us
  Pallas kernels  91.9 us (98%)
    pallas_call x1, Pallas kernels, body(): pl.pallas_call(kernel, name='sinkhorn', out_shape=[jax.ShapeDtypeStruct(s...  91.9 us

profile of v3, /device:TPU:1, one launch (start us, length us, event | category | flops | bytes accessed | tf_op | source)
XLA Modules:
  0.0 93.7 jit_solution(6531991562522878802)
XLA Ops:
  0.6 91.9 %sinkhorn.1 = (f32[3,16,128]{2,1,0:T(8,128)S(1)}, f32[8,128]{1,0:T(8,128)S(1)}) custom-call(f32[64,64]{1,0:T(8,128)} %x_hbm.1, f32[64,1024]{1,0:T(8,128)} %bitcast.7), custom_call_target="tpu_custom_call" | custom-call | tf_op jit(solution)/shard_map/sinkhorn/pallas_call | solution.py:368
  92.5 0.6 multiply_bitcast_fusion
  93.1 0.6 copy.6

commit v4 on v3

--- a/solution.py
+++ b/solution.py
@@ -22,7 +22,7 @@
 LOG_CELLS = math.log2(CELLS)
 LIFT = 30.0
 SCALE = 90.0
-FAR_HOPS = 9
+FAR_HOPS = 4
 MESH = pl.DeviceIdType.MESH
 
 
@@ -255,7 +255,7 @@
         return jnp.sum(block, 0, keepdims=True)
 
     row_max[...] = row_max[...] * kappa[0:1, :]
-    GROUP = 16
+    GROUP = 32
 
     tops = [spread(row_max, t) for t in range(ROW_TILES)]
 

time: 93.9 us -> 92.7 us (0.987)
  Pallas kernels: 91.9 us -> 90.8 us
    pallas_call x1, Pallas kernels: 91.9 us -> 90.8 us  [body(): pl.pallas_call(kernel, name='sinkhorn', out_shape=[jax.ShapeDtypeStruct(s...]
where the time goes in v4:
time: 92.7 us; the launch traced here: 92.6 us
  Pallas kernels  90.8 us (98%)
    pallas_call x1, Pallas kernels, body(): pl.pallas_call(kernel, name='sinkhorn', out_shape=[jax.ShapeDtypeStruct(s...  90.8 us

profile of v4, /device:TPU:1, one launch (start us, length us, event | category | flops | bytes accessed | tf_op | source)
XLA Modules:
  0.0 92.6 jit_solution(3452170489496671752)
XLA Ops:
  0.6 90.8 %sinkhorn.1 = (f32[3,16,128]{2,1,0:T(8,128)S(1)}, f32[8,128]{1,0:T(8,128)S(1)}) custom-call(f32[64,64]{1,0:T(8,128)} %x_hbm.1, f32[64,1024]{1,0:T(8,128)} %bitcast.7), custom_call_target="tpu_custom_call" | custom-call | tf_op jit(solution)/shard_map/sinkhorn/pallas_call | solution.py:368
  91.4 0.6 multiply_bitcast_fusion
  92.0 0.6 copy.6
